TPU v7x, 32 devices: a whole 2x2x4 slice. The times are simulated.
32 devices in a mesh: groups: 2 (over y), lat: 8 (over z, x), tp: 2 (over core).
Axes of the slice: x: 2, y: 2, z: 4, core: 2. Of those that a mesh axis runs over, the one named last changes fastest.
Arguments:
- partials: bfloat16 [2, 128, 4608], P('tp', ('groups', 'lat')), parts along dimension 1, may hold values from -5 to 5
- token_ids: int32 [128], P('groups'), parts along dimension 0, may hold values from 0 to 255999, as said below
- enc_weight: bfloat16 [3072, 4608], P('lat'), may hold values from -0.09375 to 0.09375
- enc_bias: float32 [3072], P('lat'), may hold values from -3 to 3
- dec_weight: bfloat16 [3072, 4608], P('lat'), may hold values from -0.109375 to 0.109375
Outputs:
- recon: bfloat16 [128, 4608], P(('groups', 'lat', 'tp')), parts along dimension 0
- input_grad: float32 [128, 4608], P(('groups', 'lat', 'tp')), parts along dimension 0
- grad_enc: bfloat16 [6144, 4608], P(('groups', 'lat', 'tp')), parts along dimension 0
- grad_dec: bfloat16 [6144, 4608], P(('groups', 'lat', 'tp')), parts along dimension 0
- grad_bias: float32 [6144], P(('groups', 'lat', 'tp')), parts along dimension 0
There are 2 independent parts, one for each index of `groups`. A program takes and returns all parts, laid end to end along the dimension named above; an argument that names none is the same for every part. Nothing has to cross between parts.
Inputs may be any that keep to these rules, and one draw needn't show every extreme that they name: `token_ids`: ids 0, 1 and 2 are padding, end and beginning markers; the others are ordinary tokens.
All inputs are finite; a program needn't handle non-finite values.
Results may differ from a plain program's by a relative error of at most 0.009.
Values may be sent and summed in bfloat16 or wider, within the bound.
A program may use at most 128 MiB of HBM per device.

v0:
```python
import jax
import jax.numpy as jnp
from jax import lax
from jax.sharding import PartitionSpec as P

l1_weight = 0.2


def on_device(partials, token_ids, enc_weight, enc_bias, dec_weight):
    n_lat = lax.axis_size("lat")
    n_tp = lax.axis_size("tp")
    tp_index = lax.axis_index("tp")
    lat_index = lax.axis_index("lat")
    half = partials.shape[1] // n_tp
    shard_sum = partials[0].astype(jnp.float32)
    summed = lax.psum(shard_sum.astype(jnp.bfloat16), "tp").astype(jnp.float32)
    own_rows = lax.dynamic_slice_in_dim(summed, tp_index * half, half, 0)
    own_acts = own_rows.astype(jnp.bfloat16)
    gathered = lax.all_gather(own_acts, "lat", axis=0, tiled=True)
    id_table = token_ids.reshape(n_lat, n_tp, half)
    my_ids = lax.dynamic_index_in_dim(id_table, tp_index, 1, keepdims=False).reshape(-1)
    keep = (my_ids >= 3).astype(jnp.float32)[:, None]
    pre = (
        lax.dot_general(
            gathered, enc_weight, (((1,), (1,)), ((), ())), preferred_element_type=jnp.float32
        )
        + enc_bias
    )
    act = (jax.nn.softplus(8.0 * pre) / 8.0).astype(jnp.bfloat16)
    slope = jax.nn.sigmoid(8.0 * pre)
    total = lax.psum(jnp.dot(act, dec_weight, preferred_element_type=jnp.float32), "lat")
    signal = (keep * (total - gathered.astype(jnp.float32))).astype(jnp.bfloat16)
    own_total = lax.dynamic_slice_in_dim(total, lat_index * half, half, 0)
    recon = own_total.astype(jnp.bfloat16)
    back = (
        lax.dot_general(
            signal, dec_weight, (((1,), (1,)), ((), ())), preferred_element_type=jnp.float32
        )
        + l1_weight * keep
    )
    dpre = (back * slope).astype(jnp.bfloat16)
    enc_term = lax.dot_general(
        dpre, gathered, (((0,), (0,)), ((), ())), preferred_element_type=jnp.float32
    )
    dec_term = lax.dot_general(
        act, signal, (((0,), (0,)), ((), ())), preferred_element_type=jnp.float32
    )
    bias_term = jnp.sum(dpre.astype(jnp.float32), axis=0)
    enc_grad, dec_grad, bias_grad = (
        lax.psum_scatter(
            enc_term.astype(jnp.bfloat16), "tp", scatter_dimension=0, tiled=True
        ).astype(jnp.float32),
        lax.psum_scatter(
            dec_term.astype(jnp.bfloat16), "tp", scatter_dimension=0, tiled=True
        ).astype(jnp.float32),
        lax.psum_scatter(
            bias_term.astype(jnp.bfloat16), "tp", scatter_dimension=0, tiled=True
        ).astype(jnp.float32),
    )
    inward = lax.psum_scatter(
        jnp.dot(dpre, enc_weight, preferred_element_type=jnp.float32),
        "lat",
        scatter_dimension=0,
        tiled=True,
    )
    mine_signal = lax.dynamic_slice_in_dim(signal, lat_index * half, half, 0)
    input_grad = inward - mine_signal.astype(jnp.float32)
    return (
        recon,
        input_grad,
        enc_grad.astype(jnp.bfloat16),
        dec_grad.astype(jnp.bfloat16),
        bias_grad,
    )


def solution(mesh):
    placed = (
        P("tp", ("groups", "lat"), None),
        P("groups"),
        P("lat", None),
        P("lat"),
        P("lat", None),
    )
    return jax.shard_map(
        on_device,
        mesh=mesh,
        in_specs=placed,
        out_specs=(
            P(("groups", "lat", "tp"), None),
            P(("groups", "lat", "tp"), None),
            P(("groups", "lat", "tp"), None),
            P(("groups", "lat", "tp"), None),
            P(("groups", "lat", "tp")),
        ),
        check_vma=False,
    )
```

profile of v0, /device:TPU:0, one launch (start us, length us, event | category | flops | bytes accessed | tf_op | source)
XLA Modules:
  0.0 259.3 jit_solution(13137601497515055269)
XLA Ops:
  7.2 0.0 copy-start
  7.2 0.0 all-reduce.6.cloned.1.call-start
  7.2 0.7 all-reduce.6.cloned.1.call-update
  7.9 0.0 all-reduce.8.cloned.1.call-start
  8.0 22.7 %all-reduce.6.cloned.1.call-done = bf16[8,4608]{1,0:T(8,128)(2,1)} async-done(((bf16[8,4608]{1,0:T(8,128)(2,1)}), bf16[8,4608]{1,0:T(8,128)(2,1)}) %all-reduce.6.cloned.1.call-update) | async-done | bytes 73744 | tf_op jit(solution)/shard_map/psum | solution.py:16
  30.7 0.9 fusion.5
  31.6 33.4 %all-gather = bf16[8,4,4608]{2,1,0:T(4,128)(2,1)} all-gather(bf16[1,4,4608]{2,1,0:T(4,128)(2,1)S(1)} %fusion.5), channel_id=1, replica_groups=mesh['groups'=2,'lat'=8,'tp'=2] {'lat'}, dimensions={0}, use_global_device_ids=true | all-gather | bytes 331776 | tf_op jit(solution)/shard_map/all_gather | solution.py:19
  65.0 1.7 reshape.37
  66.8 0.0 copy-start.5
  66.8 3.2 %fusion.1 = f32[32,384]{1,0:T(8,128)S(1)} fusion(bf16[32,4608]{1,0:T(8,128)(2,1)} %reshape.37, bf16[384,4608]{1,0:T(8,128)(2,1)} %param.7, f32[384]{0:T(512)} %param.8), kind=kOutput, calls=%fused_computation.5 | convolution fusion | flops 113270784 | bytes 3884544 | tf_op jit(solution)/shard_map/dot_general | solution.py:24
  70.0 0.0 copy-start.3
  70.0 0.6 copy-done.3
  70.6 0.0 copy-done
  70.6 1.5 fusion.9
  72.2 0.0 all-reduce.8.cloned.1.call-update
  72.2 0.0 all-reduce.10.cloned.1.call-start
  72.2 0.0 copy-done.5
  72.2 0.1 reshape.34
  72.4 0.1 mul.39
  72.5 0.1 reshape.35
  72.5 73.6 %all-reduce.8.cloned.1.call-done = f32[32,4608]{1,0:T(8,128)} async-done(((f32[32,4608]{1,0:T(8,128)}), f32[32,4608]{1,0:T(8,128)}) %all-reduce.8.cloned.1.call-update) | async-done | bytes 589840 | tf_op jit(solution)/shard_map/psum | solution.py:31
  146.1 0.0 copy-start.1
  146.1 1.4 multiply_convert_fusion
  147.5 0.0 copy-start.2
  147.5 0.7 copy-done.2
  148.3 2.0 fusion.11
  150.2 0.0 copy-start.4
  150.3 0.6 copy-done.4
  150.9 0.0 copy-done.1
  150.9 1.6 fusion.12
  152.5 0.0 all-reduce.10.cloned.1.call-update
  152.5 0.0 reduce-scatter.5.cloned.1.call-start
  152.5 3.9 %convolution_convert_fusion = bf16[384,4608]{1,0:T(8,128)(2,1)} fusion(bf16[32,4608]{1,0:T(8,128)(2,1)} %copy-done.2, f32[32,384]{1,0:T(8,128)} %copy-done.3), kind=kOutput, calls=%fused_computation | convolution fusion | flops 115113984 | bytes 3883008 | tf_op jit(solution)/shard_map/dot_general | solution.py:45
  156.5 0.0 reduce-scatter.5.cloned.1.call-update
  156.5 0.0 copy-start.7
  156.5 0.0 copy-start.6
  156.5 0.0 reduce-scatter.3.cloned.1.call-start
  156.6 3.8 %convolution_convert_fusion.1 = bf16[384,4608]{1,0:T(8,128)(2,1)} fusion(bf16[32,384]{1,0:T(8,128)(2,1)} %copy-done.4, bf16[32,4608]{1,0:T(8,128)(2,1)} %reshape.37), kind=kOutput, calls=%fused_computation.1 | convolution fusion | flops 115015680 | bytes 3858432 | tf_op jit(solution)/shard_map/dot_general | solution.py:42
  160.4 0.0 reduce-scatter.3.cloned.1.call-update
  160.4 0.0 copy-done.7
  160.5 0.6 dynamic-slice.2
  161.0 0.0 copy-done.6
  161.0 0.6 dynamic-slice
  162.9 2.5 all-reduce.1
  165.4 0.6 dynamic-slice_convert_fusion.1
  166.0 1.5 dynamic-slice_convert_fusion
  167.6 56.9 %all-reduce.10.cloned.1.call-done = f32[32,4608]{1,0:T(8,128)} async-done(((f32[32,4608]{1,0:T(8,128)}), f32[32,4608]{1,0:T(8,128)}) %all-reduce.10.cloned.1.call-update) | async-done | bytes 589840
  224.4 1.6 dynamic-slice_subtract_fusion
  226.1 11.4 %reduce-scatter.5.cloned.1.call-done = bf16[192,4608]{1,0:T(8,128)(2,1)} async-done(((bf16[384,4608]{1,0:T(8,128)(2,1)}), bf16[192,4608]{1,0:T(8,128)(2,1)}) %reduce-scatter.5.cloned.1.call-update) | async-done | bytes 1769488 | tf_op jit(solution)/shard_map/reduce_scatter | solution.py:53
  237.4 15.3 %reduce-scatter.3.cloned.1.call-done = bf16[192,4608]{1,0:T(8,128)(2,1)} async-done(((bf16[384,4608]{1,0:T(8,128)(2,1)}), bf16[192,4608]{1,0:T(8,128)(2,1)}) %reduce-scatter.3.cloned.1.call-update) | async-done | bytes 1769488 | tf_op jit(solution)/shard_map/reduce_scatter | solution.py:50
  (1 shorter events, 0.0 us)
Async XLA Ops:
  7.2 63.5 %copy-start = (bf16[384,4608]{1,0:T(8,128)(2,1)S(1)}, bf16[384,4608]{1,0:T(8,128)(2,1)}, u32[]{:S(2)}) copy-start(bf16[384,4608]{1,0:T(8,128)(2,1)} %param.9) | copy-start | bytes 10616836
  7.2 23.5 %all-reduce.6.cloned.1.call-start = ((), (), s32[]{:S(2)}) async-start(), calls=%async_computation.2 | async-start | bytes 147456 | tf_op jit(solution)/shard_map/psum | solution.py:16
  7.9 138.2 %all-reduce.8.cloned.1.call-start = ((), (), s32[]{:S(2)}) async-start(), calls=%async_computation.3 | async-start | bytes 1179648 | tf_op jit(solution)/shard_map/psum | solution.py:31
  66.8 5.4 %copy-start.5 = (s32[64]{0:T(128)S(1)}, s32[64]{0:T(128)}, u32[]{:S(2)}) copy-start(s32[64]{0:T(128)} %param.6) | copy-start | bytes 772
  70.0 0.6 copy-start.3
  72.2 152.3 %all-reduce.10.cloned.1.call-start = ((), (), s32[]{:S(2)}) async-start(), calls=%async_computation.6 | async-start | bytes 1179648
  146.1 4.7 %copy-start.1 = (bf16[384,4608]{1,0:T(8,128)(2,1)S(1)}, bf16[384,4608]{1,0:T(8,128)(2,1)}, u32[]{:S(2)}) copy-start(bf16[384,4608]{1,0:T(8,128)(2,1)} %param.7) | copy-start | bytes 10616836
  147.5 0.7 copy-start.2
  150.2 0.6 copy-start.4
  152.5 85.0 %reduce-scatter.5.cloned.1.call-start = ((), (), s32[]{:S(2)}) async-start(), calls=%async_computation.5 | async-start | bytes 5308416 | tf_op jit(solution)/shard_map/reduce_scatter | solution.py:53
  156.5 4.0 %copy-start.7 = (u32[32]{0:T(128)S(1)}, u32[32]{0:T(128)}, u32[]{:S(2)}) copy-start(u32[32]{0:T(128)} %constant.45) | copy-start | bytes 388
  156.5 4.5 %copy-start.6 = (u32[32]{0:T(128)S(1)}, u32[32]{0:T(128)}, u32[]{:S(2)}) copy-start(u32[32]{0:T(128)} %constant.41) | copy-start | bytes 388
  156.5 96.3 %reduce-scatter.3.cloned.1.call-start = ((), (), s32[]{:S(2)}) async-start(), calls=%async_computation.4 | async-start | bytes 5308416 | tf_op jit(solution)/shard_map/reduce_scatter | solution.py:50
Sparse Core Ops, SparseCore 0:
  10.3 20.3 all-reduce.5
  72.3 73.7 all-reduce.7
  152.6 71.7 all-reduce.9
  227.1 10.2 reduce-scatter.4
  240.2 12.5 reduce-scatter.2
where the time goes:
time: 260 us; the launch traced here: 259 us
  waiting for transfers between devices  181 us (70%)
  blocking collectives  35.9 us (14%)
  matrix products  16.1 us (6%)
  between operations  15.2 us (6%)
  local copies, waits for them, and re-layouts  6.69 us (3%)
  other arithmetic  4.59 us (2%)
    psum x1, waiting for transfers between devices, on_device(): lax.psum(jnp.dot(act, dec_weight, preferred_element_type=jnp.float32), 'l...  73.6 us
    unnamed x6, waiting for transfers between devices  57.6 us
    all_gather x1, blocking collectives, on_device(): gathered = lax.all_gather(own_acts, 'lat', axis=0, tiled=True)  33.4 us
    psum x1, waiting for transfers between devices, on_device(): summed = lax.psum(shard_sum.astype(jnp.bfloat16), 'tp').astype(jnp.float32)  22.7 us
    reduce_scatter x1, waiting for transfers between devices, on_device(): lax.psum_scatter(enc_term.astype(jnp.bfloat16), 'tp', scatter_dimension=0...  15.3 us
    reduce_scatter x1, waiting for transfers between devices, on_device(): lax.psum_scatter(dec_term.astype(jnp.bfloat16), 'tp', scatter_dimension=0...  11.4 us
  transfers between devices with their start and end apart: 5, of which 5 were waited for; matrix products, arithmetic and copies ran while one was open for 5% of the time, Pallas kernels for 0%

commit v1 on v0

v1 whole, which is shorter than its diff:
```python
import functools

import jax
import jax.numpy as jnp
from jax import lax
from jax.experimental import pallas as pl
from jax.experimental.pallas import tpu as pltpu
from jax.sharding import PartitionSpec as P

L1_WEIGHT = 0.2
f32, bf16 = jnp.float32, jnp.bfloat16
NEAR = 2


def kernel(
    far, tokens, lats, width,
    part_ref, ids_ref, enc_hbm, bias_ref, dec_hbm,
    recon_ref, igrad_ref, genc_hbm, gdec_hbm, gbias_ref,
    enc, dec, genc, gdec,
    part, part_in, acts_all, signal_all, acts, signal,
    outgoing, pair_in, near_out, near_in, far_out, far_in, swap, swap_wide,
    load_sem, store_sem, pair_sems, ag_far, ag_near, ag_core, rs_core, rs_near, rs_far, swap_sems,
):
    quarter = width // 4
    half = width // 2
    lat = lax.axis_index("lat")
    core = lax.axis_index("tp")
    other = 1 - core
    a, b = lat // NEAR, lat % NEAR
    nb = 1 - b

    def fars(k, sign):
        return lax.rem(a + sign * k + far, far)

    def send(src, dst, sems, index, to_lat, to_core):
        copy = pltpu.make_async_remote_copy(
            src_ref=src,
            dst_ref=dst,
            send_sem=sems.at[(0, *index)],
            recv_sem=sems.at[(1, *index)],
            device_id={"lat": to_lat, "tp": to_core},
            device_id_type=pl.DeviceIdType.MESH,
        )
        copy.start()
        return copy

    loads = []
    for i, (hbm, vmem) in enumerate(((enc_hbm, enc), (dec_hbm, dec))):
        copy = pltpu.make_async_copy(
            hbm.at[pl.ds(pl.multiple_of(core * lats, lats), lats), :], vmem, load_sem.at[i]
        )
        copy.start()
        loads.append(copy)

    barrier = pltpu.get_barrier_semaphore()
    peers = [(lat, other), (a * NEAR + nb, core)]
    peers += [(fars(k, 1) * NEAR + b, core) for k in range(1, far)]
    for to_lat, to_core in peers:
        pl.semaphore_signal(
            barrier, inc=1, device_id={"lat": to_lat, "tp": to_core},
            device_id_type=pl.DeviceIdType.MESH,
        )

    mine = part_ref[0].astype(f32)
    for h in range(2):
        part[h] = jnp.concatenate(
            [mine[:, h * half:h * half + quarter], mine[:, h * half + quarter:(h + 1) * half]], axis=0
        ).astype(bf16)

    keep_row = (ids_ref[...] >= 3).astype(f32)

    def keep_column(rows, token_of):
        at = lax.broadcasted_iota(jnp.int32, (rows, tokens), 1)
        row = lax.broadcasted_iota(jnp.int32, (rows, tokens), 0)
        return jnp.sum(jnp.where(at == token_of(row), keep_row, 0.0), axis=1, keepdims=True)

    keep = keep_column(tokens, lambda i: (((i // 8) % far) * NEAR + (i // 8) // far) * 8 + i % 8)
    keep_mine = keep_column(16, lambda i: lat * 8 + i % 8)

    pl.semaphore_wait(barrier, len(peers))

    def gather(turn, ref, beside=None):
        mine_at = ref.at[core, b, a]
        sent = [
            send(mine_at, mine_at, ag_far, (turn, k), fars(k, 1) * NEAR + b, core)
            for k in range(1, far)
        ]
        near_copies, core_copies = [], []
        for k in range(far):
            origin = fars(k, -1)
            if k > 0:
                sent[k - 1].wait_recv()
            block = ref.at[core, b, origin]
            near_copies.append(send(block, block, ag_near, (turn, k), a * NEAR + nb, core))
            core_copies.append(send(block, block, ag_core, (turn, k), lat, other))
        if beside is not None:
            beside()
        for k in range(far):
            near_copies[k].wait_recv()
            block = ref.at[core, nb, fars(k, -1)]
            core_copies.append(send(block, block, ag_core, (turn, far + k), lat, other))
        for copy in core_copies:
            copy.wait_recv()
        for copy in sent + near_copies + core_copies:
            copy.wait_send()

    def unpack(ref, out):
        for h in range(2):
            blocks = ref[h].astype(f32).reshape(NEAR * far, 16, quarter)
            for s in range(2):
                out[2 * h + s] = (
                    blocks[:, 8 * s:8 * s + 8, :].reshape(tokens, quarter).astype(bf16)
                )

    def contribution(left, weight, h):
        pieces = []
        for s in range(2):
            columns = pl.ds(pl.multiple_of(h * half + s * quarter, 128), quarter)
            piece = jnp.dot(left, weight[:, columns], preferred_element_type=f32)
            pieces.append(piece.reshape(NEAR, far, 8, quarter))
        outgoing[h] = jnp.concatenate(pieces, axis=2).astype(bf16)

    def scatter(turn, left, weight, beside):
        contribution(left, weight, other)
        first = [
            send(outgoing.at[other, side], pair_in.at[turn, side], rs_core, (turn, i), lat, other)
            for i, side in enumerate((nb, b))
        ]
        contribution(left, weight, core)
        first[0].wait_recv()
        near_copies = []
        for k in [*range(1, far), 0]:
            to = fars(k, 1)
            near_out[to] = (
                outgoing[core, nb, to].astype(f32) + pair_in[turn, nb, to].astype(f32)
            ).astype(bf16)
            near_copies.append(
                send(near_out.at[to], near_in.at[turn, to], rs_near, (turn, k), a * NEAR + nb, core)
            )
        beside[0]()
        first[1].wait_recv()
        far_copies = []
        for k in [*range(1, far), 0]:
            to = fars(k, 1)
            near_copies[k - 1 if k > 0 else far - 1].wait_recv()
            summed = (
                outgoing[core, b, to].astype(f32)
                + pair_in[turn, b, to].astype(f32)
                + near_in[turn, to].astype(f32)
            )
            if k > 0:
                far_out[k] = summed.astype(bf16)
                far_copies.append(
                    send(far_out.at[k], far_in.at[turn, k], rs_far, (turn, k), to * NEAR + b, core)
                )
        beside[1]()
        for k in range(1, far):
            far_copies[k - 1].wait_recv()
            summed = summed + far_in[turn, k].astype(f32)
        for copy in first + near_copies + far_copies:
            copy.wait_send()
        return summed

    pair = send(part.at[other], part_in, pair_sems, (), lat, other)
    pair.wait_recv()
    acts_all[core, b, a] = (part[core].astype(f32) + part_in[...].astype(f32)).astype(bf16)
    gather(0, acts_all, loads[0].wait)
    pair.wait_send()
    unpack(acts_all, acts)

    def against(matrix, weight):
        total = None
        for q in range(4):
            term = lax.dot_general(
                matrix[q], weight[:, q * quarter:(q + 1) * quarter],
                (((1,), (1,)), ((), ())), preferred_element_type=f32,
            )
            total = term if total is None else total + term
        return total

    bias = jnp.where(core == 0, bias_ref[:, :lats], bias_ref[:, lats:])
    eight = 8.0 * (against(acts, enc) + bias)
    small = jnp.exp(-jnp.abs(eight))
    act = ((jnp.maximum(eight, 0.0) + jnp.log1p(small)) / 8.0).astype(bf16)
    slope = jnp.where(eight >= 0, 1.0, small) / (1.0 + small)

    def nothing():
        pass

    loads[1].wait()
    total = scatter(0, act, dec, (nothing, nothing))
    signal_mine = (keep_mine * (total - acts_all[core, b, a].astype(f32))).astype(bf16)
    signal_all[core, b, a] = signal_mine

    recon_copies = []

    def send_recon():
        swap[core] = total.astype(bf16)
        recon_copies.append(send(swap.at[core], swap.at[core], swap_sems, (0,), lat, other))

    gather(1, signal_all, send_recon)
    unpack(signal_all, signal)

    back = against(signal, dec) + L1_WEIGHT * keep
    dpre = (back * slope).astype(bf16)
    stores = []

    def gradient(left, matrix, vmem, hbm, index):
        for q in range(4):
            columns = slice(q * quarter, (q + 1) * quarter)
            vmem[:, columns] = lax.dot_general(
                left, matrix[q], (((0,), (0,)), ((), ())), preferred_element_type=f32
            ).astype(bf16)
        copy = pltpu.make_async_copy(vmem, hbm, store_sem.at[index])
        copy.start()
        stores.append(copy)

    def enc_side():
        gradient(dpre, acts, genc, genc_hbm, 0)

    def own_rows(pair):
        for h in range(2):
            for s in range(2):
                block = pair[h][8 * s:8 * s + 8].astype(f32)
                yield (2 * h + s) * quarter, jnp.where(core == 0, block[:4], block[4:])

    def dec_side():
        gradient(act, signal, gdec, gdec_hbm, 1)
        gbias_ref[...] = jnp.sum(dpre.astype(f32), axis=0, keepdims=True)
        recon_copies[0].wait_recv()
        for at, rows in own_rows(swap):
            recon_ref[:, at:at + quarter] = rows.astype(bf16)

    inward = scatter(1, dpre, enc, (enc_side, dec_side))
    swap_wide[core] = inward - signal_mine.astype(f32)
    last = send(swap_wide.at[core], swap_wide.at[core], swap_sems, (1,), lat, other)
    last.wait_recv()
    for at, rows in own_rows(swap_wide):
        igrad_ref[:, at:at + quarter] = rows
    last.wait_send()
    recon_copies[0].wait_send()
    for copy in stores:
        copy.wait()


def on_device(partials, token_ids, enc_weight, enc_bias, dec_weight):
    n_lat = lax.axis_size("lat")
    far = n_lat // NEAR
    tokens = token_ids.shape[0]
    width = enc_weight.shape[1]
    lats = enc_weight.shape[0] // 2
    quarter = width // 4
    vmem = pl.BlockSpec(memory_space=pltpu.VMEM)
    hbm = pl.BlockSpec(memory_space=pl.ANY)
    dma = pltpu.SemaphoreType.DMA
    flops = 2 * 6 * tokens * lats * width
    recon, igrad, genc, gdec, gbias = pl.pallas_call(
        functools.partial(kernel, far, tokens, lats, width),
        out_shape=(
            jax.ShapeDtypeStruct((4, width), bf16),
            jax.ShapeDtypeStruct((4, width), f32),
            jax.ShapeDtypeStruct((lats, width), bf16),
            jax.ShapeDtypeStruct((lats, width), bf16),
            jax.ShapeDtypeStruct((1, lats), f32),
        ),
        in_specs=[vmem, vmem, hbm, vmem, hbm],
        out_specs=(vmem, vmem, hbm, hbm, vmem),
        scratch_shapes=[
            pltpu.VMEM((lats, width), bf16),
            pltpu.VMEM((lats, width), bf16),
            pltpu.VMEM((lats, width), bf16),
            pltpu.VMEM((lats, width), bf16),
            pltpu.VMEM((2, 16, quarter), bf16),
            pltpu.VMEM((16, quarter), bf16),
            pltpu.VMEM((2, NEAR, far, 16, quarter), bf16),
            pltpu.VMEM((2, NEAR, far, 16, quarter), bf16),
            pltpu.VMEM((4, tokens, quarter), bf16),
            pltpu.VMEM((4, tokens, quarter), bf16),
            pltpu.VMEM((2, NEAR, far, 16, quarter), bf16),
            pltpu.VMEM((2, NEAR, far, 16, quarter), bf16),
            pltpu.VMEM((far, 16, quarter), bf16),
            pltpu.VMEM((2, far, 16, quarter), bf16),
            pltpu.VMEM((far, 16, quarter), bf16),
            pltpu.VMEM((2, far, 16, quarter), bf16),
            pltpu.VMEM((2, 16, quarter), bf16),
            pltpu.VMEM((2, 16, quarter), f32),
            dma((2,)),
            dma((2,)),
            dma((2,)),
            dma((2, 2, far)),
            dma((2, 2, far)),
            dma((2, 2, 2 * far)),
            dma((2, 2, 2)),
            dma((2, 2, far)),
            dma((2, 2, far)),
            dma((2, 2)),
        ],
        compiler_params=pltpu.CompilerParams(
            collective_id=0, has_side_effects=True, vmem_limit_bytes=60 * 2**20
        ),
        cost_estimate=pl.CostEstimate(
            flops=flops, bytes_accessed=8 * lats * width, transcendentals=4 * tokens * lats
        ),
    )(partials, token_ids.reshape(1, -1), enc_weight, enc_bias.reshape(1, -1), dec_weight)
    return recon, igrad, genc, gdec, gbias.reshape(-1)


def solution(mesh):
    placed = (
        P("tp", ("groups", "lat"), None),
        P("groups"),
        P("lat", None),
        P("lat"),
        P("lat", None),
    )
    split = P(("groups", "lat", "tp"), None)
    return jax.shard_map(
        on_device,
        mesh=mesh,
        in_specs=placed,
        out_specs=(split, split, split, split, P(("groups", "lat", "tp"))),
        check_vma=False,
    )
```

time: 260 us -> 57.8 us (0.22)
  waiting for transfers between devices: 181 us -> 0 us
  Pallas kernels: 0 us -> 48 us
  blocking collectives: 35.9 us -> 0 us
  matrix products: 16.1 us -> 0 us
  between operations: 15.2 us -> 0.64 us
  other arithmetic: 4.59 us -> 0 us
    psum x2 -> x0, waiting for transfers between devices: 96.3 us -> none  [the longest x1 73.6 us: on_device(): lax.psum(jnp.dot(act, dec_weight, preferred_element_type=jnp.float32), 'l...]
    unnamed x6 -> x0, waiting for transfers between devices: 57.6 us -> none
    pallas_call x0 -> x1, Pallas kernels: none -> 48 us  [on_device(): pl.pallas_call(functools.partial(kernel, far, tokens, lats, width), out_s...]
    all_gather x1 -> x0, blocking collectives: 33.4 us -> none  [on_device(): gathered = lax.all_gather(own_acts, 'lat', axis=0, tiled=True)]
    reduce_scatter x2 -> x0, waiting for transfers between devices: 26.7 us -> none  [the longest x1 15.3 us: on_device(): lax.psum_scatter(enc_term.astype(jnp.bfloat16), 'tp', scatter_dimension=0...]
    dot_general x6 -> x0, matrix products: 16.1 us -> none  [the longest x1 3.93 us: on_device(): lax.dot_general(act, signal, (((0,), (0,)), ((), ())), preferred_element_...]
    unnamed x19 -> x9, local copies, waits for them, and re-layouts: 4.9 us -> 7.62 us
  transfers between devices with their start and end apart: 5 -> 0, of which waited for: 5 -> 0; matrix products, arithmetic and copies ran while one was open for 5% -> 0% of each run, Pallas kernels for 0% -> 0%
where the time goes in v1:
time: 57.8 us; the launch traced here: 57.5 us
  Pallas kernels  48 us (83%)
  local copies, waits for them, and re-layouts  8.87 us (15%)
  between operations  0.64 us (1%)
    pallas_call x1, Pallas kernels, on_device(): pl.pallas_call(functools.partial(kernel, far, tokens, lats, width), out_s...  48 us
    unnamed x9, local copies, waits for them, and re-layouts  7.62 us
    reshape x1, local copies, waits for them, and re-layouts, on_device(): enc_bias.reshape(1, -1)  1.25 us

profile of v1, /device:TPU:0, one launch (start us, length us, event | category | flops | bytes accessed | tf_op | source)
XLA Modules:
  0.0 57.5 jit_solution(8140444879062257701)
XLA Ops:
  0.6 1.2 %reshape.20.bias_ref = f32[1,384]{1,0:T(1,128)} reshape(f32[384]{0:T(512)} %param.8) | data formatting | bytes 3072 | tf_op jit(solution)/shard_map/reshape | solution.py:304
  1.9 48.0 %shard_map.92 = (bf16[4,4608]{1,0:T(4,128)(2,1)}, f32[4,4608]{1,0:T(4,128)}, bf16[192,4608]{1,0:T(8,128)(2,1)}, bf16[192,4608]{1,0:T(8,128)(2,1)}, f32[1,192]{1,0:T(1,128)}) custom-call(bf16[1,8,4608]{2,1,0:T(8,128)(2,1)} %part_ref.1, s32[1,64]{1,0:T(1,128)} %bitcast.3, bf16[384,4608]{1,0:T(8,128)(2,1)} %enc_hbm.1, f32[1,384]{1,0:T(1,128)} %reshape.20.bias_ref, ...), custom_call_target="tpu_custom_call" | custom-call | flops 679477248 | bytes 7077888 | tf_op jit(solution)/shard_map/pallas_call | solution.py:257
  49.9 1.4 %copy.15 = bf16[4,4608]{1,0:T(4,128)(2,1)} copy(bf16[4,4608]{1,0:T(4,128)(2,1)} %get-tuple-element.20) | data formatting | bytes 73728
  51.3 1.5 %copy.16 = f32[4,4608]{1,0:T(4,128)} copy(f32[4,4608]{1,0:T(4,128)} %get-tuple-element.21) | data formatting | bytes 147456
  52.8 0.0 copy-start
  52.8 2.9 %copy.17 = bf16[192,4608]{1,0:T(8,128)(2,1)} copy(bf16[192,4608]{1,0:T(8,128)(2,1)} %get-tuple-element.22) | data formatting | bytes 3538944
  55.8 0.0 copy-done
  55.8 0.0 copy-start.1
  55.8 1.2 %copy.18 = bf16[192,4608]{1,0:T(8,128)(2,1)} copy(bf16[192,4608]{1,0:T(8,128)(2,1)S(1)} %copy-done) | data formatting | bytes 3538944
  57.0 0.0 copy-done.1
  57.0 0.6 copy.19
Async XLA Ops:
  52.8 2.9 %copy-start = (bf16[192,4608]{1,0:T(8,128)(2,1)S(1)}, bf16[192,4608]{1,0:T(8,128)(2,1)}, u32[]{:S(2)}) copy-start(bf16[192,4608]{1,0:T(8,128)(2,1)} %get-tuple-element.23) | copy-start | bytes 5308420
  55.8 1.2 %copy-start.1 = (f32[1,192]{1,0:T(1,128)S(1)}, f32[1,192]{1,0:T(1,128)}, u32[]{:S(2)}) copy-start(f32[1,192]{1,0:T(1,128)} %get-tuple-element.14) | copy-start | bytes 2308

commit v2 on v1

--- a/solution.py
+++ b/solution.py
@@ -18,11 +18,10 @@
     recon_ref, igrad_ref, genc_hbm, gdec_hbm, gbias_ref,
     enc, dec, genc, gdec,
     part, part_in, acts_all, signal_all, acts, signal,
-    outgoing, pair_in, near_out, near_in, far_out, far_in, swap, swap_wide,
-    load_sem, store_sem, pair_sems, ag_far, ag_near, ag_core, rs_core, rs_near, rs_far, swap_sems,
+    outgoing, plane_in, far_out, far_in,
+    load_sem, store_sem, pair_sems, ag_far, ag_plane, rs_plane, rs_far,
 ):
     quarter = width // 4
-    half = width // 2
     lat = lax.axis_index("lat")
     core = lax.axis_index("tp")
     other = 1 - core
@@ -53,7 +52,8 @@
         loads.append(copy)
 
     barrier = pltpu.get_barrier_semaphore()
-    peers = [(lat, other), (a * NEAR + nb, core)]
+    plane = [(nb, core), (nb, other), (b, other)]
+    peers = [(a * NEAR + near, k) for near, k in plane]
     peers += [(fars(k, 1) * NEAR + b, core) for k in range(1, far)]
     for to_lat, to_core in peers:
         pl.semaphore_signal(
@@ -62,10 +62,9 @@
         )
 
     mine = part_ref[0].astype(f32)
-    for h in range(2):
-        part[h] = jnp.concatenate(
-            [mine[:, h * half:h * half + quarter], mine[:, h * half + quarter:(h + 1) * half]], axis=0
-        ).astype(bf16)
+    quarters = [mine[:, q * quarter:(q + 1) * quarter] for q in range(4)]
+    for k in range(2):
+        part[k] = jnp.concatenate([v[4 * k:4 * k + 4] for v in quarters], axis=0).astype(bf16)
 
     keep_row = (ids_ref[...] >= 3).astype(f32)
 
@@ -75,7 +74,7 @@
         return jnp.sum(jnp.where(at == token_of(row), keep_row, 0.0), axis=1, keepdims=True)
 
     keep = keep_column(tokens, lambda i: (((i // 8) % far) * NEAR + (i // 8) // far) * 8 + i % 8)
-    keep_mine = keep_column(16, lambda i: lat * 8 + i % 8)
+    keep_mine = keep_column(16, lambda i: lat * 8 + core * 4 + i % 4)
 
     pl.semaphore_wait(barrier, len(peers))
 
@@ -85,69 +84,58 @@
             send(mine_at, mine_at, ag_far, (turn, k), fars(k, 1) * NEAR + b, core)
             for k in range(1, far)
         ]
-        near_copies, core_copies = [], []
+        passed = []
         for k in range(far):
-            origin = fars(k, -1)
             if k > 0:
                 sent[k - 1].wait_recv()
-            block = ref.at[core, b, origin]
-            near_copies.append(send(block, block, ag_near, (turn, k), a * NEAR + nb, core))
-            core_copies.append(send(block, block, ag_core, (turn, k), lat, other))
-        if beside is not None:
-            beside()
-        for k in range(far):
-            near_copies[k].wait_recv()
-            block = ref.at[core, nb, fars(k, -1)]
-            core_copies.append(send(block, block, ag_core, (turn, far + k), lat, other))
-        for copy in core_copies:
+            block = ref.at[core, b, fars(k, -1)]
+            for slot, (near, to_core) in enumerate(plane):
+                passed.append(
+                    send(block, block, ag_plane, (turn, slot, k), a * NEAR + near, to_core)
+                )
+            if k == 0 and beside is not None:
+                beside()
+        for copy in passed:
             copy.wait_recv()
-        for copy in sent + near_copies + core_copies:
+        for copy in sent + passed:
             copy.wait_send()
 
     def unpack(ref, out):
-        for h in range(2):
-            blocks = ref[h].astype(f32).reshape(NEAR * far, 16, quarter)
-            for s in range(2):
-                out[2 * h + s] = (
-                    blocks[:, 8 * s:8 * s + 8, :].reshape(tokens, quarter).astype(bf16)
+        halves = [ref[k].astype(f32).reshape(NEAR * far, 16, quarter) for k in range(2)]
+        for q in range(4):
+            out[q] = (
+                jnp.concatenate([v[:, 4 * q:4 * q + 4, :] for v in halves], axis=1)
+                .reshape(tokens, quarter)
+                .astype(bf16)
+            )
+
+    def scatter(turn, left, weight, beside):
+        pieces = [
+            jnp.dot(
+                left, weight[:, q * quarter:(q + 1) * quarter], preferred_element_type=f32
+            ).reshape(NEAR * far, 8, quarter)
+            for q in range(4)
+        ]
+        for k in range(2):
+            rows = jnp.concatenate([v[:, 4 * k:4 * k + 4, :] for v in pieces], axis=1)
+            outgoing[k] = rows.astype(bf16).reshape(NEAR, far, 16, quarter)
+        order = [*range(1, far), 0]
+        first = {}
+        for k in order:
+            to = fars(k, 1)
+            for slot, (near, to_core) in enumerate(plane):
+                first[slot, k] = send(
+                    outgoing.at[to_core, near, to], plane_in.at[turn, slot, to],
+                    rs_plane, (turn, slot, k), a * NEAR + near, to_core,
                 )
-
-    def contribution(left, weight, h):
-        pieces = []
-        for s in range(2):
-            columns = pl.ds(pl.multiple_of(h * half + s * quarter, 128), quarter)
-            piece = jnp.dot(left, weight[:, columns], preferred_element_type=f32)
-            pieces.append(piece.reshape(NEAR, far, 8, quarter))
-        outgoing[h] = jnp.concatenate(pieces, axis=2).astype(bf16)
-
-    def scatter(turn, left, weight, beside):
-        contribution(left, weight, other)
-        first = [
-            send(outgoing.at[other, side], pair_in.at[turn, side], rs_core, (turn, i), lat, other)
-            for i, side in enumerate((nb, b))
-        ]
-        contribution(left, weight, core)
-        first[0].wait_recv()
-        near_copies = []
-        for k in [*range(1, far), 0]:
+        beside[0]()
+        far_copies = []
+        for k in order:
             to = fars(k, 1)
-            near_out[to] = (
-                outgoing[core, nb, to].astype(f32) + pair_in[turn, nb, to].astype(f32)
-            ).astype(bf16)
-            near_copies.append(
-                send(near_out.at[to], near_in.at[turn, to], rs_near, (turn, k), a * NEAR + nb, core)
-            )
-        beside[0]()
-        first[1].wait_recv()
-        far_copies = []
-        for k in [*range(1, far), 0]:
-            to = fars(k, 1)
-            near_copies[k - 1 if k > 0 else far - 1].wait_recv()
-            summed = (
-                outgoing[core, b, to].astype(f32)
-                + pair_in[turn, b, to].astype(f32)
-                + near_in[turn, to].astype(f32)
-            )
+            summed = outgoing[core, b, to].astype(f32)
+            for slot in range(3):
+                first[slot, k].wait_recv()
+                summed = summed + plane_in[turn, slot, to].astype(f32)
             if k > 0:
                 far_out[k] = summed.astype(bf16)
                 far_copies.append(
@@ -157,7 +145,7 @@
         for k in range(1, far):
             far_copies[k - 1].wait_recv()
             summed = summed + far_in[turn, k].astype(f32)
-        for copy in first + near_copies + far_copies:
+        for copy in [*first.values(), *far_copies]:
             copy.wait_send()
         return summed
 
@@ -192,13 +180,11 @@
     signal_mine = (keep_mine * (total - acts_all[core, b, a].astype(f32))).astype(bf16)
     signal_all[core, b, a] = signal_mine
 
-    recon_copies = []
-
-    def send_recon():
-        swap[core] = total.astype(bf16)
-        recon_copies.append(send(swap.at[core], swap.at[core], swap_sems, (0,), lat, other))
-
-    gather(1, signal_all, send_recon)
+    def write_recon():
+        for q in range(4):
+            recon_ref[:, q * quarter:(q + 1) * quarter] = total[4 * q:4 * q + 4].astype(bf16)
+
+    gather(1, signal_all, write_recon)
     unpack(signal_all, signal)
 
     back = against(signal, dec) + L1_WEIGHT * keep
@@ -218,28 +204,34 @@
     def enc_side():
         gradient(dpre, acts, genc, genc_hbm, 0)
 
-    def own_rows(pair):
-        for h in range(2):
-            for s in range(2):
-                block = pair[h][8 * s:8 * s + 8].astype(f32)
-                yield (2 * h + s) * quarter, jnp.where(core == 0, block[:4], block[4:])
-
     def dec_side():
         gradient(act, signal, gdec, gdec_hbm, 1)
         gbias_ref[...] = jnp.sum(dpre.astype(f32), axis=0, keepdims=True)
-        recon_copies[0].wait_recv()
-        for at, rows in own_rows(swap):
-            recon_ref[:, at:at + quarter] = rows.astype(bf16)
 
     inward = scatter(1, dpre, enc, (enc_side, dec_side))
-    swap_wide[core] = inward - signal_mine.astype(f32)
-    last = send(swap_wide.at[core], swap_wide.at[core], swap_sems, (1,), lat, other)
-    last.wait_recv()
-    for at, rows in own_rows(swap_wide):
-        igrad_ref[:, at:at + quarter] = rows
-    last.wait_send()
-    recon_copies[0].wait_send()
+    inward = inward - signal_mine.astype(f32)
+    for q in range(4):
+        igrad_ref[:, q * quarter:(q + 1) * quarter] = inward[4 * q:4 * q + 4]
     for copy in stores:
+        copy.wait()
+
+
+def deliver(
+    parts, recon_in, igrad_in, genc_in, gdec_in, gbias_in, recon, igrad, genc, gdec, gbias, sems
+):
+    copies = []
+    for source, target in ((genc_in, genc), (gdec_in, gdec)):
+        rows = source.shape[0] // parts
+        for i in range(parts):
+            at = pl.ds(i * rows, rows)
+            copies.append((source.at[at, :], target.at[at, :]))
+    copies += [(recon_in, recon), (igrad_in, igrad), (gbias_in, gbias)]
+    started = []
+    for i, (source, target) in enumerate(copies):
+        copy = pltpu.make_async_copy(source, target, sems.at[i])
+        copy.start()
+        started.append(copy)
+    for copy in started:
         copy.wait()
 
 
@@ -277,23 +269,16 @@
             pltpu.VMEM((4, tokens, quarter), bf16),
             pltpu.VMEM((4, tokens, quarter), bf16),
             pltpu.VMEM((2, NEAR, far, 16, quarter), bf16),
-            pltpu.VMEM((2, NEAR, far, 16, quarter), bf16),
+            pltpu.VMEM((2, 3, far, 16, quarter), bf16),
             pltpu.VMEM((far, 16, quarter), bf16),
             pltpu.VMEM((2, far, 16, quarter), bf16),
-            pltpu.VMEM((far, 16, quarter), bf16),
-            pltpu.VMEM((2, far, 16, quarter), bf16),
-            pltpu.VMEM((2, 16, quarter), bf16),
-            pltpu.VMEM((2, 16, quarter), f32),
             dma((2,)),
             dma((2,)),
             dma((2,)),
             dma((2, 2, far)),
+            dma((2, 2, 3, far)),
+            dma((2, 2, 3, far)),
             dma((2, 2, far)),
-            dma((2, 2, 2 * far)),
-            dma((2, 2, 2)),
-            dma((2, 2, far)),
-            dma((2, 2, far)),
-            dma((2, 2)),
         ],
         compiler_params=pltpu.CompilerParams(
             collective_id=0, has_side_effects=True, vmem_limit_bytes=60 * 2**20
@@ -302,6 +287,18 @@
             flops=flops, bytes_accessed=8 * lats * width, transcendentals=4 * tokens * lats
         ),
     )(partials, token_ids.reshape(1, -1), enc_weight, enc_bias.reshape(1, -1), dec_weight)
+    made = (recon, igrad, genc, gdec, gbias)
+    recon, igrad, genc, gdec, gbias = pl.pallas_call(
+        functools.partial(deliver, 4),
+        out_shape=tuple(jax.ShapeDtypeStruct(x.shape, x.dtype) for x in made),
+        in_specs=[hbm] * 5,
+        out_specs=(hbm,) * 5,
+        scratch_shapes=[dma((11,))],
+        compiler_params=pltpu.CompilerParams(vmem_limit_bytes=60 * 2**20),
+        cost_estimate=pl.CostEstimate(
+            flops=0, bytes_accessed=8 * lats * width, transcendentals=0
+        ),
+    )(*made)
     return recon, igrad, genc, gdec, gbias.reshape(-1)
 
 

time: 57.8 us -> 165 us (2.85)
  Pallas kernels: 48 us -> 163 us
  local copies, waits for them, and re-layouts: 8.87 us -> 1.25 us
    pallas_call x0 -> x1, Pallas kernels: none -> 112 us  [on_device(): pl.pallas_call(functools.partial(deliver, 4), out_shape=tuple((jax.ShapeD...]
    unnamed x9 -> x0, local copies, waits for them, and re-layouts: 7.62 us -> none
    pallas_call x1, Pallas kernels: 48 us -> 51.6 us  [on_device(): pl.pallas_call(functools.partial(kernel, far, tokens, lats, width), out_s...]
where the time goes in v2:
time: 165 us
  Pallas kernels  163 us (99%)
    pallas_call x1, Pallas kernels, on_device(): pl.pallas_call(functools.partial(deliver, 4), out_shape=tuple((jax.ShapeD...  112 us
    pallas_call x1, Pallas kernels, on_device(): pl.pallas_call(functools.partial(kernel, far, tokens, lats, width), out_s...  51.6 us

profile of v2, /device:TPU:0, one launch (start us, length us, event | category | flops | bytes accessed | tf_op | source)
XLA Modules:
  0.0 165.2 jit_solution(7503350684328847595)
XLA Ops:
  0.6 1.2 reshape.20.bias_ref
  1.9 51.6 %shard_map.92 = (bf16[4,4608]{1,0:T(4,128)(2,1)}, f32[4,4608]{1,0:T(4,128)}, bf16[192,4608]{1,0:T(8,128)(2,1)}, bf16[192,4608]{1,0:T(8,128)(2,1)}, f32[1,192]{1,0:T(1,128)}) custom-call(bf16[1,8,4608]{2,1,0:T(8,128)(2,1)} %part_ref.1, s32[1,64]{1,0:T(1,128)} %bitcast.2, bf16[384,4608]{1,0:T(8,128)(2,1)} %enc_hbm.1, f32[1,384]{1,0:T(1,128)} %reshape.20.bias_ref, ...), custom_call_target="tpu_custom_call" | custom-call | flops 679477248 | bytes 7077888 | tf_op jit(solution)/shard_map/pallas_call | solution.py:249
  53.4 111.8 %shard_map.93 = (bf16[4,4608]{1,0:T(4,128)(2,1)}, f32[4,4608]{1,0:T(4,128)}, bf16[192,4608]{1,0:T(8,128)(2,1)}, bf16[192,4608]{1,0:T(8,128)(2,1)}, f32[1,192]{1,0:T(1,128)}) custom-call(bf16[4,4608]{1,0:T(4,128)(2,1)} %get-tuple-element.15.recon_in, f32[4,4608]{1,0:T(4,128)} %get-tuple-element.16.igrad_in, bf16[192,4608]{1,0:T(8,128)(2,1)} %get-tuple-element.17.genc_in, ...), custom_call_target="tpu_custom_call" | custom-call | bytes 7077888 | tf_op jit(solution)/shard_map/pallas_call | solution.py:291

commit v3 on v1

--- a/solution.py
+++ b/solution.py
@@ -15,14 +15,13 @@
 def kernel(
     far, tokens, lats, width,
     part_ref, ids_ref, enc_hbm, bias_ref, dec_hbm,
-    recon_ref, igrad_ref, genc_hbm, gdec_hbm, gbias_ref,
-    enc, dec, genc, gdec,
+    recon_ref, igrad_ref, acts_hbm, signal_hbm, act_ref, dpre_ref,
+    enc, dec,
     part, part_in, acts_all, signal_all, acts, signal,
-    outgoing, pair_in, near_out, near_in, far_out, far_in, swap, swap_wide,
-    load_sem, store_sem, pair_sems, ag_far, ag_near, ag_core, rs_core, rs_near, rs_far, swap_sems,
+    outgoing, pair_in, near_out, near_in, far_out, far_in,
+    load_sem, store_sem, pair_sems, ag_far, ag_near, ag_core, rs_core, rs_near, rs_far,
 ):
     quarter = width // 4
-    half = width // 2
     lat = lax.axis_index("lat")
     core = lax.axis_index("tp")
     other = 1 - core
@@ -62,10 +61,9 @@
         )
 
     mine = part_ref[0].astype(f32)
-    for h in range(2):
-        part[h] = jnp.concatenate(
-            [mine[:, h * half:h * half + quarter], mine[:, h * half + quarter:(h + 1) * half]], axis=0
-        ).astype(bf16)
+    quarters = [mine[:, q * quarter:(q + 1) * quarter] for q in range(4)]
+    for k in range(2):
+        part[k] = jnp.concatenate([v[4 * k:4 * k + 4] for v in quarters], axis=0).astype(bf16)
 
     keep_row = (ids_ref[...] >= 3).astype(f32)
 
@@ -75,7 +73,7 @@
         return jnp.sum(jnp.where(at == token_of(row), keep_row, 0.0), axis=1, keepdims=True)
 
     keep = keep_column(tokens, lambda i: (((i // 8) % far) * NEAR + (i // 8) // far) * 8 + i % 8)
-    keep_mine = keep_column(16, lambda i: lat * 8 + i % 8)
+    keep_mine = keep_column(16, lambda i: lat * 8 + core * 4 + i % 4)
 
     pl.semaphore_wait(barrier, len(peers))
 
@@ -105,28 +103,28 @@
             copy.wait_send()
 
     def unpack(ref, out):
-        for h in range(2):
-            blocks = ref[h].astype(f32).reshape(NEAR * far, 16, quarter)
-            for s in range(2):
-                out[2 * h + s] = (
-                    blocks[:, 8 * s:8 * s + 8, :].reshape(tokens, quarter).astype(bf16)
-                )
-
-    def contribution(left, weight, h):
-        pieces = []
-        for s in range(2):
-            columns = pl.ds(pl.multiple_of(h * half + s * quarter, 128), quarter)
-            piece = jnp.dot(left, weight[:, columns], preferred_element_type=f32)
-            pieces.append(piece.reshape(NEAR, far, 8, quarter))
-        outgoing[h] = jnp.concatenate(pieces, axis=2).astype(bf16)
+        halves = [ref[k].astype(f32).reshape(NEAR * far, 16, quarter) for k in range(2)]
+        for q in range(4):
+            out[q] = (
+                jnp.concatenate([v[:, 4 * q:4 * q + 4, :] for v in halves], axis=1)
+                .reshape(tokens, quarter)
+                .astype(bf16)
+            )
 
     def scatter(turn, left, weight, beside):
-        contribution(left, weight, other)
+        pieces = [
+            jnp.dot(
+                left, weight[:, q * quarter:(q + 1) * quarter], preferred_element_type=f32
+            ).reshape(NEAR * far, 8, quarter)
+            for q in range(4)
+        ]
+        for k in range(2):
+            rows = jnp.concatenate([v[:, 4 * k:4 * k + 4, :] for v in pieces], axis=1)
+            outgoing[k] = rows.astype(bf16).reshape(NEAR, far, 16, quarter)
         first = [
             send(outgoing.at[other, side], pair_in.at[turn, side], rs_core, (turn, i), lat, other)
             for i, side in enumerate((nb, b))
         ]
-        contribution(left, weight, core)
         first[0].wait_recv()
         near_copies = []
         for k in [*range(1, far), 0]:
@@ -178,7 +176,8 @@
             total = term if total is None else total + term
         return total
 
-    bias = jnp.where(core == 0, bias_ref[:, :lats], bias_ref[:, lats:])
+    both = bias_ref[...].reshape(1, -1)
+    bias = jnp.where(core == 0, both[:, :lats], both[:, lats:])
     eight = 8.0 * (against(acts, enc) + bias)
     small = jnp.exp(-jnp.abs(eight))
     act = ((jnp.maximum(eight, 0.0) + jnp.log1p(small)) / 8.0).astype(bf16)
@@ -192,55 +191,45 @@
     signal_mine = (keep_mine * (total - acts_all[core, b, a].astype(f32))).astype(bf16)
     signal_all[core, b, a] = signal_mine
 
-    recon_copies = []
-
-    def send_recon():
-        swap[core] = total.astype(bf16)
-        recon_copies.append(send(swap.at[core], swap.at[core], swap_sems, (0,), lat, other))
-
-    gather(1, signal_all, send_recon)
+    def write_recon():
+        for q in range(4):
+            recon_ref[:, q * quarter:(q + 1) * quarter] = total[4 * q:4 * q + 4].astype(bf16)
+
+    gather(1, signal_all, write_recon)
     unpack(signal_all, signal)
 
     back = against(signal, dec) + L1_WEIGHT * keep
     dpre = (back * slope).astype(bf16)
-    stores = []
-
-    def gradient(left, matrix, vmem, hbm, index):
-        for q in range(4):
-            columns = slice(q * quarter, (q + 1) * quarter)
-            vmem[:, columns] = lax.dot_general(
-                left, matrix[q], (((0,), (0,)), ((), ())), preferred_element_type=f32
-            ).astype(bf16)
-        copy = pltpu.make_async_copy(vmem, hbm, store_sem.at[index])
+    act_ref[...] = act
+    dpre_ref[...] = dpre
+
+    def store(matrix, hbm, index):
+        copy = pltpu.make_async_copy(matrix, hbm, store_sem.at[index])
         copy.start()
-        stores.append(copy)
-
-    def enc_side():
-        gradient(dpre, acts, genc, genc_hbm, 0)
-
-    def own_rows(pair):
-        for h in range(2):
-            for s in range(2):
-                block = pair[h][8 * s:8 * s + 8].astype(f32)
-                yield (2 * h + s) * quarter, jnp.where(core == 0, block[:4], block[4:])
-
-    def dec_side():
-        gradient(act, signal, gdec, gdec_hbm, 1)
-        gbias_ref[...] = jnp.sum(dpre.astype(f32), axis=0, keepdims=True)
-        recon_copies[0].wait_recv()
-        for at, rows in own_rows(swap):
-            recon_ref[:, at:at + quarter] = rows.astype(bf16)
-
-    inward = scatter(1, dpre, enc, (enc_side, dec_side))
-    swap_wide[core] = inward - signal_mine.astype(f32)
-    last = send(swap_wide.at[core], swap_wide.at[core], swap_sems, (1,), lat, other)
-    last.wait_recv()
-    for at, rows in own_rows(swap_wide):
-        igrad_ref[:, at:at + quarter] = rows
-    last.wait_send()
-    recon_copies[0].wait_send()
+        return copy
+
+    stores = [store(acts, acts_hbm, 0), store(signal, signal_hbm, 1)]
+    inward = scatter(1, dpre, enc, (nothing, nothing))
+    inward = inward - signal_mine.astype(f32)
+    for q in range(4):
+        igrad_ref[:, q * quarter:(q + 1) * quarter] = inward[4 * q:4 * q + 4]
     for copy in stores:
         copy.wait()
+
+
+def gradients(
+    acts, signal, act, dpre, recon_in, igrad_in, recon, igrad, genc, gdec, gbias
+):
+    for left, right, out in ((dpre, acts, genc), (act, signal, gdec)):
+        out[...] = lax.dot_general(
+            left[...], right[0], (((0,), (0,)), ((), ())), preferred_element_type=f32
+        ).astype(bf16)
+
+    @pl.when(pl.program_id(0) == 0)
+    def _():
+        recon[...] = recon_in[...]
+        igrad[...] = igrad_in[...]
+        gbias[...] = jnp.sum(dpre[...].astype(f32), axis=0, keepdims=True)
 
 
 def on_device(partials, token_ids, enc_weight, enc_bias, dec_weight):
@@ -254,20 +243,19 @@
     hbm = pl.BlockSpec(memory_space=pl.ANY)
     dma = pltpu.SemaphoreType.DMA
     flops = 2 * 6 * tokens * lats * width
-    recon, igrad, genc, gdec, gbias = pl.pallas_call(
+    recon, igrad, acts, signal, act, dpre = pl.pallas_call(
         functools.partial(kernel, far, tokens, lats, width),
         out_shape=(
             jax.ShapeDtypeStruct((4, width), bf16),
             jax.ShapeDtypeStruct((4, width), f32),
-            jax.ShapeDtypeStruct((lats, width), bf16),
-            jax.ShapeDtypeStruct((lats, width), bf16),
-            jax.ShapeDtypeStruct((1, lats), f32),
+            jax.ShapeDtypeStruct((4, tokens, quarter), bf16),
+            jax.ShapeDtypeStruct((4, tokens, quarter), bf16),
+            jax.ShapeDtypeStruct((tokens, lats), bf16),
+            jax.ShapeDtypeStruct((tokens, lats), bf16),
         ),
         in_specs=[vmem, vmem, hbm, vmem, hbm],
-        out_specs=(vmem, vmem, hbm, hbm, vmem),
+        out_specs=(vmem, vmem, hbm, hbm, vmem, vmem),
         scratch_shapes=[
-            pltpu.VMEM((lats, width), bf16),
-            pltpu.VMEM((lats, width), bf16),
             pltpu.VMEM((lats, width), bf16),
             pltpu.VMEM((lats, width), bf16),
             pltpu.VMEM((2, 16, quarter), bf16),
@@ -282,8 +270,6 @@
             pltpu.VMEM((2, far, 16, quarter), bf16),
             pltpu.VMEM((far, 16, quarter), bf16),
             pltpu.VMEM((2, far, 16, quarter), bf16),
-            pltpu.VMEM((2, 16, quarter), bf16),
-            pltpu.VMEM((2, 16, quarter), f32),
             dma((2,)),
             dma((2,)),
             dma((2,)),
@@ -293,7 +279,6 @@
             dma((2, 2, 2)),
             dma((2, 2, far)),
             dma((2, 2, far)),
-            dma((2, 2)),
         ],
         compiler_params=pltpu.CompilerParams(
             collective_id=0, has_side_effects=True, vmem_limit_bytes=60 * 2**20
@@ -301,7 +286,35 @@
         cost_estimate=pl.CostEstimate(
             flops=flops, bytes_accessed=8 * lats * width, transcendentals=4 * tokens * lats
         ),
-    )(partials, token_ids.reshape(1, -1), enc_weight, enc_bias.reshape(1, -1), dec_weight)
+    )(partials, token_ids.reshape(1, -1), enc_weight, enc_bias, dec_weight)
+
+    def whole(*shape):
+        return pl.BlockSpec(shape, lambda i: (0,) * len(shape))
+
+    by_tokens = pl.BlockSpec((1, tokens, quarter), lambda i: (i, 0, 0))
+    by_lats = pl.BlockSpec((lats, quarter), lambda i: (0, i))
+    recon, igrad, genc, gdec, gbias = pl.pallas_call(
+        gradients,
+        grid=(4,),
+        out_shape=(
+            jax.ShapeDtypeStruct((4, width), bf16),
+            jax.ShapeDtypeStruct((4, width), f32),
+            jax.ShapeDtypeStruct((lats, width), bf16),
+            jax.ShapeDtypeStruct((lats, width), bf16),
+            jax.ShapeDtypeStruct((1, lats), f32),
+        ),
+        in_specs=[
+            by_tokens, by_tokens, whole(tokens, lats), whole(tokens, lats),
+            whole(4, width), whole(4, width),
+        ],
+        out_specs=(whole(4, width), whole(4, width), by_lats, by_lats, whole(1, lats)),
+        compiler_params=pltpu.CompilerParams(vmem_limit_bytes=60 * 2**20),
+        cost_estimate=pl.CostEstimate(
+            flops=4 * tokens * lats * width,
+            bytes_accessed=4 * (lats + tokens) * width,
+            transcendentals=0,
+        ),
+    )(acts, signal, act, dpre, recon, igrad)
     return recon, igrad, genc, gdec, gbias.reshape(-1)
 
 

time: 57.8 us -> 53.4 us (0.924)
  local copies, waits for them, and re-layouts: 8.87 us -> 0 us
  Pallas kernels: 48 us -> 52.5 us
    unnamed x9 -> x0, local copies, waits for them, and re-layouts: 7.62 us -> none
    pallas_call x0 -> x1, Pallas kernels: none -> 4.82 us  [on_device(): pl.pallas_call(gradients, grid=(4,), out_shape=(jax.ShapeDtypeStruct((4,...]
    reshape x1 -> x0, local copies, waits for them, and re-layouts: 1.25 us -> none  [on_device(): enc_bias.reshape(1, -1)]
where the time goes in v3:
time: 53.4 us; the launch traced here: 53.2 us
  Pallas kernels  52.5 us (98%)
  between operations  0.64 us (1%)
    pallas_call x1, Pallas kernels, on_device(): pl.pallas_call(functools.partial(kernel, far, tokens, lats, width), out_s...  47.7 us
    pallas_call x1, Pallas kernels, on_device(): pl.pallas_call(gradients, grid=(4,), out_shape=(jax.ShapeDtypeStruct((4,...  4.82 us

profile of v3, /device:TPU:0, one launch (start us, length us, event | category | flops | bytes accessed | tf_op | source)
XLA Modules:
  0.0 53.2 jit_solution(3262926762049917748)
XLA Ops:
  0.6 47.7 %shard_map.92 = (bf16[4,4608]{1,0:T(4,128)(2,1)}, f32[4,4608]{1,0:T(4,128)}, bf16[4,64,1152]{2,1,0:T(8,128)(2,1)}, bf16[4,64,1152]{2,1,0:T(8,128)(2,1)}, bf16[64...) custom-call(bf16[1,8,4608]{2,1,0:T(8,128)(2,1)} %part_ref.1, s32[1,64]{1,0:T(1,128)} %bitcast.2, bf16[384,4608]{1,0:T(8,128)(2,1)} %enc_hbm.1, ...), custom_call_target="tpu_custom_call" | custom-call | flops 679477248 | bytes 7077888 | tf_op jit(solution)/shard_map/pallas_call | solution.py:246
  48.3 4.8 %shard_map.93 = (bf16[4,4608]{1,0:T(4,128)(2,1)}, f32[4,4608]{1,0:T(4,128)}, bf16[192,4608]{1,0:T(8,128)(2,1)}, bf16[192,4608]{1,0:T(8,128)(2,1)}, f32[1,192]{1,0:T(1,128)}) custom-call(bf16[4,64,1152]{2,1,0:T(8,128)(2,1)} %get-tuple-element.16.acts, bf16[4,64,1152]{2,1,0:T(8,128)(2,1)} %get-tuple-element.17.signal, bf16[64,192]{1,0:T(8,128)(2,1)} %get-tuple-element.18.act, ...), custom_call_target="tpu_custom_call" | custom-call | flops 226492416 | bytes 4718592 | tf_op jit(solution)/shard_map/pallas_call | solution.py:296
